TPU v7x, 32 devices: a whole 2x2x4 slice. The times are simulated.
32 devices in a mesh: fsdp: 16 (over z, y, x), replica: 2 (over core).
Axes of the slice: x: 2, y: 2, z: 4, core: 2. Of those that a mesh axis runs over, the one named last changes fastest.
Arguments:
- partials: float32 [2, 16384, 128], P('replica', 'fsdp'), may hold values from -6 to 6
- diag_stat: float32 [16384, 128], P('fsdp'), may hold values from 0.8 to 3
- first_stat: float32 [16384, 128], P('fsdp'), may hold values from -0.35 to 0.35
- second_stat: float32 [16384, 128], P('fsdp'), may hold values from -0.35 to 0.35
Outputs:
- update: float32 [16384, 128], P('fsdp')
- diag_next: float32 [16384, 128], P('fsdp')
- first_next: float32 [16384, 128], P('fsdp')
- second_next: float32 [16384, 128], P('fsdp')
All inputs are finite; a program needn't handle non-finite values.
Results may differ from a plain program's by a relative error of at most 0.00002.
Values sent between devices are 32-bit elements; how exact they have to be, the bound alone decides.
No kernel may reach another device: no remote copies, remote signals or barrier semaphores. Data moves between devices by JAX's collectives and lax.ppermute only.
A program may use at most 64 MiB of HBM per device.

v0:
```python
import jax
import jax.numpy as jnp
from jax import lax
from jax.sharding import PartitionSpec as P

decay_rate = 0.95
damping = 0.01


def shifted(block, axis, distance):
    devices = range(lax.axis_size(axis))
    route = [(i - distance, i) for i in devices if i - distance in devices]
    return lax.ppermute(block, axis, route)


def precondition(
    gradient, diag_stat, first_stat, second_stat, first_row, total_rows, send_next, send_prev
):
    count = gradient.shape[0]
    width = gradient.shape[1]
    head_diag = decay_rate * diag_stat[:2] + gradient[:2] * gradient[:2]
    head_first = decay_rate * first_stat[:2] + gradient[:2] * gradient[1:3]
    received = send_next(jnp.stack([gradient[:2], head_diag, head_first]))
    row_index = first_row + lax.broadcasted_iota(jnp.int32, (count + 2, width), 0)
    local_index = row_index[:count]
    grad_ext = jnp.concatenate([gradient, received[0]], axis=0)
    diag_next = decay_rate * diag_stat + gradient * gradient
    first_next = jnp.where(
        local_index < total_rows - 1,
        decay_rate * first_stat + gradient * grad_ext[1 : count + 1],
        0.0,
    )
    second_next = jnp.where(
        local_index < total_rows - 2,
        decay_rate * second_stat + gradient * grad_ext[2 : count + 2],
        0.0,
    )
    damped = jnp.where(
        row_index < total_rows, jnp.concatenate([diag_next, received[1]], axis=0) + damping, 1.0
    )
    first_ext = jnp.concatenate([first_next, received[2]], axis=0)
    upper_diag = damped[1 : count + 1]
    lower_diag = damped[2 : count + 2]
    coupling = first_ext[1 : count + 1]
    determinant = upper_diag * lower_diag - coupling * coupling
    first_coef = (lower_diag * first_next - coupling * second_next) / determinant
    second_coef = (upper_diag * second_next - coupling * first_next) / determinant
    schur = damped[:count] - first_next * first_coef - second_next * second_coef
    value = (
        gradient - first_coef * grad_ext[1 : count + 1] - second_coef * grad_ext[2 : count + 2]
    ) / schur
    earlier = send_prev(jnp.stack([value[-2:], first_coef[-2:], second_coef[-2:]]))
    value_ext = jnp.concatenate([earlier[0], value], axis=0)
    first_prev = jnp.concatenate([earlier[1], first_coef], axis=0)
    second_prev = jnp.concatenate([earlier[2], second_coef], axis=0)
    update = (
        value
        - first_prev[1 : count + 1] * value_ext[1 : count + 1]
        - second_prev[0:count] * value_ext[0:count]
    )
    return (update, diag_next, first_next, second_next)


def body(partials, diag_stat, first_stat, second_stat):
    own_part = partials[0]
    summed = lax.psum(own_part, "replica")
    gradient = summed / lax.axis_size("replica")
    count = gradient.shape[0]
    first_row = lax.axis_index("fsdp") * count
    total_rows = count * lax.axis_size("fsdp")

    def send_next(stacked):
        return shifted(stacked, "fsdp", -1)

    def send_prev(stacked):
        return shifted(stacked, "fsdp", 1)

    return precondition(
        gradient, diag_stat, first_stat, second_stat, first_row, total_rows, send_next, send_prev
    )


def solution(mesh):
    return jax.shard_map(
        body,
        mesh=mesh,
        in_specs=(P("replica", "fsdp", None), P("fsdp", None), P("fsdp", None), P("fsdp", None)),
        out_specs=(P("fsdp", None), P("fsdp", None), P("fsdp", None), P("fsdp", None)),
        check_vma=False,
    )
```

profile of v0, /device:TPU:8, one launch (start us, length us, event | category | flops | bytes accessed | tf_op | source)
XLA Modules:
  0.0 55.7 jit_solution(2365004975343080533)
XLA Ops:
  7.2 0.0 copy-start.3
  7.2 0.0 all-reduce.2.cloned.1.call-start
  7.2 0.7 %all-reduce.2.cloned.1.call-update = ((f32[1024,128]{1,0:T(8,128)}), f32[1024,128]{1,0:T(8,128)}) async-update(((), (), s32[]{:S(2)}) %all-reduce.2.cloned.1.call-start, f32[1024,128]{1,0:T(8,128)} %bitcast.25) | async-update | bytes 1572888
  7.9 0.0 copy-start.2
  8.0 22.6 %all-reduce.2.cloned.1.call-done = f32[1024,128]{1,0:T(8,128)} async-done(((f32[1024,128]{1,0:T(8,128)}), f32[1024,128]{1,0:T(8,128)}) %all-reduce.2.cloned.1.call-update) | async-done | bytes 524304 | tf_op jit(solution)/shard_map/psum | solution.py:66
  30.5 0.0 copy-done.3
  30.5 1.1 %multiply_add_fusion = (f32[1024,128]{1,0:T(8,128)S(1)}, f32[1024,128]{1,0:T(8,128)S(1)}) fusion(f32[1024,128]{1,0:T(8,128)S(1)} %copy-done.3, f32[1024,128]{1,0:T(8,128)} %all-reduce.2.cloned.1.call-done), kind=kLoop, calls=%fused_computation.34 | loop fusion | flops 524288 | bytes 2097152 | tf_op jit(solution)/shard_map/add | solution.py:27
  31.7 0.0 copy-start
  31.7 0.0 copy-done.2
  31.7 4.3 %collective-permute-start = (f32[3,2,128]{2,1,0:T(2,128)S(1)}, f32[3,2,128]{2,1,0:T(2,128)S(1)}, u32[]{:S(2)}, u32[]{:S(2)}) collective-permute-start(f32[3,2,128]{2,1,0:T(2,128)S(1)} %pad_maximum_fusion.5), channel_id=1, source_target_pairs={{2,0},{4,2},{6,4},{8,6},{10,8},{12,10},{14,12},{16,14},{18,16},{20... | collective-permute-start | bytes 9224 | tf_op jit(solution)/shard_map/ppermute | solution.py:13
  36.0 1.3 %collective-permute-done = f32[3,2,128]{2,1,0:T(2,128)S(1)} collective-permute-done((f32[3,2,128]{2,1,0:T(2,128)S(1)}, f32[3,2,128]{2,1,0:T(2,128)S(1)}, u32[]{:S(2)}, u32[]{:S(2)}) %collective-permute-start) | collective-permute-done | bytes 3104 | tf_op jit(solution)/shard_map/ppermute | solution.py:13
  37.3 0.2 add_select_fusion
  37.5 0.0 copy-start.1
  37.5 0.0 copy-done
  37.5 0.0 copy-start.4
  37.5 0.2 fusion
  37.8 0.6 copy-done.1
  38.3 0.5 copy-done.4
  38.8 1.5 %fusion.8 = (f32[1024,128]{1,0:T(8,128)S(1)}, f32[1024,128]{1,0:T(8,128)S(1)}, f32[1024,128]{1,0:T(8,128)S(1)}, f32[1024,128]{1,0:T(8,128)}) fusion(f32[1026,128]{1,0:T(8,128)S(1)} %fusion, f32[2,128]{1,0:T(2,128)S(1)} %get-tuple-element.19, f32[1024,128]{1,0:T(8,128)S(1)} %get-tuple-element.9, f32[1024,128]{1,0:T(8,128)S(1)} %add_select_fusion, ...), kind=kLoop, calls=%fused_computation.17 | loop fusion | flops 3538944 | bytes 5245952 | tf_op jit(solution)/shard_map/div | solution.py:49
  40.3 4.2 %collective-permute-start.1 = (f32[3,2,128]{2,1,0:T(2,128)S(1)}, f32[3,2,128]{2,1,0:T(2,128)S(1)}, u32[]{:S(2)}, u32[]{:S(2)}) collective-permute-start(f32[3,2,128]{2,1,0:T(2,128)S(1)} %pad_maximum_fusion.6), channel_id=1, source_target_pairs={{0,2},{2,4},{4,6},{6,8},{8,10},{10,12},{12,14},{14,16},{16,18},{18... | collective-permute-start | bytes 9224 | tf_op jit(solution)/shard_map/ppermute | solution.py:13
  44.5 3.3 %collective-permute-done.1 = f32[3,2,128]{2,1,0:T(2,128)S(1)} collective-permute-done((f32[3,2,128]{2,1,0:T(2,128)S(1)}, f32[3,2,128]{2,1,0:T(2,128)S(1)}, u32[]{:S(2)}, u32[]{:S(2)}) %collective-permute-start.1) | collective-permute-done | bytes 3104 | tf_op jit(solution)/shard_map/ppermute | solution.py:13
  47.8 1.0 %fusion.4 = f32[1024,128]{1,0:T(8,128)} fusion(f32[1024,128]{1,0:T(8,128)S(1)} %get-tuple-element.4, f32[2,128]{1,0:T(2,128)S(1)} %get-tuple-element.17, f32[1024,128]{1,0:T(8,128)S(1)} %get-tuple-element.6, f32[2,128]{1,0:T(2,128)S(1)} %get-tuple-element.16, f32[1024,128]{1,0:T(8,128)S(1)} %get-tuple-element.5, f32[2,128]{1,0:T(2,128)S(1)} %get-tuple-element.15), kind=kLoop, calls=%fused_computation.9 | loop fusion | flops 1048576 | bytes 2100224 | tf_op jit(solution)/shard_map/sub | solution.py:57
  (10 shorter events, 0.1 us)
Async XLA Ops:
  7.2 23.4 %copy-start.3 = (f32[1024,128]{1,0:T(8,128)S(1)}, f32[1024,128]{1,0:T(8,128)}, u32[]{:S(2)}) copy-start(f32[1024,128]{1,0:T(8,128)} %param.5) | copy-start | bytes 1572868
  7.2 23.4 %all-reduce.2.cloned.1.call-start = ((), (), s32[]{:S(2)}) async-start(), calls=%async_computation | async-start | bytes 1048576 | tf_op jit(solution)/shard_map/psum | solution.py:66
  7.9 23.7 %copy-start.2 = (f32[1024,128]{1,0:T(8,128)S(1)}, f32[1024,128]{1,0:T(8,128)}, u32[]{:S(2)}) copy-start(f32[1024,128]{1,0:T(8,128)} %param.6) | copy-start | bytes 1572868
  31.7 5.9 %copy-start = (f32[1024,128]{1,0:T(8,128)}, f32[1024,128]{1,0:T(8,128)S(1)}, u32[]{:S(2)}) copy-start(f32[1024,128]{1,0:T(8,128)S(1)} %get-tuple-element.8) | copy-start | bytes 1572868
  31.7 5.6 %collective-permute-start = (f32[3,2,128]{2,1,0:T(2,128)S(1)}, f32[3,2,128]{2,1,0:T(2,128)S(1)}, u32[]{:S(2)}, u32[]{:S(2)}) collective-permute-start(f32[3,2,128]{2,1,0:T(2,128)S(1)} %pad_maximum_fusion.5), channel_id=1, source_target_pairs={{2,0},{4,2},{6,4},{8,6},{10,8},{12,10},{14,12},{16,14},{18,16},{20... | collective-permute-start | bytes 9224 | tf_op jit(solution)/shard_map/ppermute | solution.py:13
  37.5 0.8 %copy-start.1 = (f32[1024,128]{1,0:T(8,128)}, f32[1024,128]{1,0:T(8,128)S(1)}, u32[]{:S(2)}) copy-start(f32[1024,128]{1,0:T(8,128)S(1)} %add_select_fusion) | copy-start | bytes 1572868
  37.5 1.2 %copy-start.4 = (f32[1024,128]{1,0:T(8,128)S(1)}, f32[1024,128]{1,0:T(8,128)}, u32[]{:S(2)}) copy-start(f32[1024,128]{1,0:T(8,128)} %param.7) | copy-start | bytes 1572868
  40.3 7.6 %collective-permute-start.1 = (f32[3,2,128]{2,1,0:T(2,128)S(1)}, f32[3,2,128]{2,1,0:T(2,128)S(1)}, u32[]{:S(2)}, u32[]{:S(2)}) collective-permute-start(f32[3,2,128]{2,1,0:T(2,128)S(1)} %pad_maximum_fusion.6), channel_id=1, source_target_pairs={{0,2},{2,4},{4,6},{6,8},{8,10},{10,12},{12,14},{14,16},{16,18},{18... | collective-permute-start | bytes 9224 | tf_op jit(solution)/shard_map/ppermute | solution.py:13
Sparse Core Ops, SparseCore 0:
  10.3 20.1 all-reduce.1
where the time goes:
time: 55.9 us; the launch traced here: 55.7 us
  waiting for transfers between devices  27.9 us (50%)
  between operations  14.2 us (25%)
  starting transfers between devices  8.5 us (15%)
  other arithmetic  4.04 us (7%)
  local copies, waits for them, and re-layouts  1.05 us (2%)
    psum x1, waiting for transfers between devices, body(): summed = lax.psum(own_part, 'replica')  22.6 us
    ppermute x2, starting transfers between devices, shifted(): return lax.ppermute(block, axis, route)  8.46 us
    ppermute x2, waiting for transfers between devices, shifted(): return lax.ppermute(block, axis, route)  4.63 us
    div x1, other arithmetic, precondition(): (gradient - first_coef * grad_ext[1:count + 1] - second_coef * grad_ext[2...  1.46 us
    add x1, other arithmetic, precondition(): diag_next = decay_rate * diag_stat + gradient * gradient  1.12 us
  transfers between devices with their start and end apart: 3, of which 3 were waited for; matrix products, arithmetic and copies ran while one was open for 0% of the time, Pallas kernels for 0%

commit v1 on v0

v1 whole, which is shorter than its diff:
```python
import functools

import jax
import jax.numpy as jnp
from jax import lax
from jax.experimental import pallas as pl
from jax.experimental.pallas import tpu as pltpu
from jax.sharding import PartitionSpec as P

decay_rate = 0.95
damping = 0.01
PAD = 8


def kernel(
    parts, scale, rows, step,
    *refs,
):
    own = refs[:parts]
    diag_ref, first_ref, second_ref = refs[parts : parts + 3]
    before = refs[parts + 3 : 2 * parts + 3]
    after = refs[2 * parts + 3 : 3 * parts + 3]
    outs = refs[3 * parts + 3 : 3 * parts + 7]
    grad, diag, first, second, value, part1, part2, update, sems = refs[3 * parts + 7 :]
    width = diag_ref.shape[1]
    chunks = rows // step
    end = PAD + rows

    def total(pieces):
        out = pieces[0]
        for piece in pieces[1:]:
            out = out + piece
        return out * scale

    g_lo = total([r[0:2, :] for r in before])
    g_hi = total([r[0:2, :] for r in after])
    present = after[0][6:8, :]
    grad[PAD - 2 : PAD, :] = g_lo
    grad[end : end + 2, :] = g_hi
    diag[PAD - 2 : PAD, :] = decay_rate * before[0][2:4, :] + g_lo * g_lo
    diag[end : end + 2, :] = (
        decay_rate * after[0][2:4, :] + g_hi * g_hi + (1.0 - present) * (1.0 - damping)
    )

    def gradients(c, carry):
        at = pl.multiple_of(c * step, step)
        here = pl.ds(at, step)
        there = pl.ds(at + PAD, step)
        g = total([r[here, :] for r in own])
        grad[there, :] = g
        diag[there, :] = decay_rate * diag_ref[here, :] + g * g
        return carry

    lax.fori_loop(0, chunks, gradients, 0, unroll=True)

    def bands(c, carry):
        at = pl.multiple_of(c * step, step)
        here = pl.ds(at, step)
        g = grad[pl.ds(at + PAD, step), :]
        first[pl.ds(at + PAD, step), :] = (
            decay_rate * first_ref[here, :] + g * grad[pl.ds(at + PAD + 1, step), :]
        )
        second[pl.ds(at + PAD, step), :] = (
            decay_rate * second_ref[here, :] + g * grad[pl.ds(at + PAD + 2, step), :]
        )
        return carry

    lax.fori_loop(0, chunks, bands, 0, unroll=True)
    first[PAD - 2 : PAD, :] = (
        decay_rate * before[0][4:6, :] + g_lo * grad[PAD - 1 : PAD + 1, :]
    )
    second[PAD - 2 : PAD, :] = (
        decay_rate * before[0][6:8, :] + g_lo * grad[PAD : PAD + 2, :]
    )
    first[end - 1 : end, :] = first[end - 1 : end, :] * present[0:1, :]
    second[end - 2 : end, :] = second[end - 2 : end, :] * present
    first[end : end + 1, :] = (
        decay_rate * after[0][4:5, :] + g_hi[0:1, :] * g_hi[1:2, :]
    )

    copies = []

    def send(scratch, k):
        copy = pltpu.make_async_copy(scratch.at[PAD:end, :], outs[k], sems.at[k])
        copy.start()
        copies.append(copy)

    send(diag, 1)
    send(first, 2)
    send(second, 3)

    def solve(at, size):
        g = grad[pl.ds(at, size), :]
        g1 = grad[pl.ds(at + 1, size), :]
        g2 = grad[pl.ds(at + 2, size), :]
        d = diag[pl.ds(at, size), :] + damping
        upper = diag[pl.ds(at + 1, size), :] + damping
        lower = diag[pl.ds(at + 2, size), :] + damping
        f = first[pl.ds(at, size), :]
        c = first[pl.ds(at + 1, size), :]
        s = second[pl.ds(at, size), :]
        det = upper * lower - c * c
        n1 = lower * f - c * s
        n2 = upper * s - c * f
        schur = d * det - f * n1 - s * n2
        top = g * det - n1 * g1 - n2 * g2
        w = top / (schur * det)
        return w * det, w * n1, w * n2

    _, p1, p2 = solve(PAD - 2, 2)
    part1[PAD - 2 : PAD, :] = p1
    part2[PAD - 2 : PAD, :] = p2

    def values(c, carry):
        at = pl.multiple_of(c * step, step)
        v, p1, p2 = solve(at + PAD, step)
        there = pl.ds(at + PAD, step)
        part1[there, :] = p1
        part2[there, :] = p2
        update[pl.ds(at, step), :] = (
            v - part1[pl.ds(at + PAD - 1, step), :] - part2[pl.ds(at + PAD - 2, step), :]
        )
        return carry

    lax.fori_loop(0, chunks, values, 0, unroll=True)
    copy = pltpu.make_async_copy(update, outs[0], sems.at[0])
    copy.start()
    copies.append(copy)
    for copy in copies:
        copy.wait()


def body(partials, diag_stat, first_stat, second_stat):
    own = partials[0]
    rows, width = own.shape
    replicas = lax.axis_size("replica")
    shards = lax.axis_size("fsdp")
    scale = 1.0 / replicas
    axes = ("fsdp", "replica")

    def route(distance, turn):
        return [
            (i * replicas + r, (i + distance) * replicas + (r + turn) % replicas)
            for i in range(shards)
            for r in range(replicas)
            if 0 <= i + distance < shards
        ]

    if replicas > 2:
        own = lax.psum(own, "replica")
        turns = [0]
    else:
        turns = list(range(replicas))

    last = jnp.concatenate([own[-2:], diag_stat[-2:], first_stat[-2:], second_stat[-2:]])
    head = jnp.concatenate(
        [own[:2], diag_stat[:2], first_stat[:2], jnp.ones((2, width), jnp.float32)]
    )
    before = [
        lax.ppermute(last if t == 0 else own[-2:], axes, route(1, t)) for t in turns
    ]
    after = [
        lax.ppermute(head if t == 0 else own[:2], axes, route(-1, t)) for t in turns
    ]
    pieces = [own if t == 0 else lax.ppermute(own, axes, route(0, t)) for t in turns]
    parts = len(pieces)

    shape = jax.ShapeDtypeStruct((rows, width), jnp.float32)
    vmem = pl.BlockSpec(memory_space=pltpu.VMEM)
    hbm = pl.BlockSpec(memory_space=pl.ANY)
    padded = pltpu.VMEM((rows + 2 * PAD, width), jnp.float32)
    step = 64 if rows % 64 == 0 else 8
    return pl.pallas_call(
        functools.partial(kernel, parts, scale, rows, step),
        out_shape=(shape,) * 4,
        in_specs=[vmem] * (3 * parts + 3),
        out_specs=(hbm,) * 4,
        scratch_shapes=[padded] * 7
        + [pltpu.VMEM((rows, width), jnp.float32), pltpu.SemaphoreType.DMA((4,))],
        compiler_params=pltpu.CompilerParams(vmem_limit_bytes=24 * 2**20),
        name="precondition",
    )(*pieces, diag_stat, first_stat, second_stat, *before, *after)


def solution(mesh):
    return jax.shard_map(
        body,
        mesh=mesh,
        in_specs=(P("replica", "fsdp", None), P("fsdp", None), P("fsdp", None), P("fsdp", None)),
        out_specs=(P("fsdp", None), P("fsdp", None), P("fsdp", None), P("fsdp", None)),
        check_vma=False,
    )
```

time: 55.9 us -> 26.4 us (0.47)
  the two profiles are of different devices: /device:TPU:8 before, /device:TPU:9 now
where the time goes in v1:
time: 26.4 us; the launch traced here: 26 us
  starting transfers between devices  13.4 us (51%)
  local copies, waits for them, and re-layouts  6.37 us (24%)
  waiting for transfers between devices  3.74 us (14%)
  Pallas kernels  1.69 us (6%)
  between operations  0.7 us (3%)
    ppermute x2, starting transfers between devices, body(): lax.ppermute(head if t == 0 else own[:2], axes, route(-1, t))  6.58 us
    ppermute x2, starting transfers between devices, body(): lax.ppermute(last if t == 0 else own[-2:], axes, route(1, t))  6.05 us
    unnamed x8, local copies, waits for them, and re-layouts  4.16 us
    ppermute x2, waiting for transfers between devices, body(): lax.ppermute(last if t == 0 else own[-2:], axes, route(1, t))  3.73 us
    pallas_call x1, Pallas kernels, body(): pl.pallas_call(functools.partial(kernel, parts, scale, rows, step), out_s...  1.69 us
    ppermute x1, starting transfers between devices, body(): lax.ppermute(own, axes, route(0, t))  0.74 us
    slice x1, local copies, waits for them, and re-layouts, body(): diag_stat[:2]  0.74 us
    slice x1, local copies, waits for them, and re-layouts, body(): own[:2]  0.71 us
  transfers between devices with their start and end apart: 5, of which 1 were waited for; matrix products, arithmetic and copies ran while one was open for 9% of the time, Pallas kernels for 0%

profile of v1, /device:TPU:9, one launch (start us, length us, event | category | flops | bytes accessed | tf_op | source)
XLA Modules:
  0.0 26.0 jit_solution(16718222679004440419)
XLA Ops:
  0.6 0.7 %collective-permute-start = (f32[1024,128]{1,0:T(8,128)}, f32[1024,128]{1,0:T(8,128)S(1)}, u32[]{:S(2)}, u32[]{:S(2)}) collective-permute-start(f32[1024,128]{1,0:T(8,128)} %bitcast.5), channel_id=1, source_target_pairs={{0,1},{1,0},{2,3},{3,2},{4,5},{5,4},{6,7},{7,6},{8,9},{9,8},{10,11... | collective-permute-start | bytes 1572872 | tf_op jit(solution)/shard_map/ppermute | solution.py:165
  1.4 0.7 %slice.33 = f32[2,128]{1,0:T(2,128)S(1)} slice(f32[1024,128]{1,0:T(8,128)} %refs_4_.1), slice={[1022:1024], [0:128]} | slice | bytes 2048 | tf_op jit(solution)/shard_map/slice | solution.py:155
  2.1 0.7 %fusion = (f32[2,128]{1,0:T(2,128)S(1)}, f32[2,128]{1,0:T(2,128)S(1)}, f32[2,128]{1,0:T(2,128)S(1)}, f32[2,128]{1,0:T(2,128)S(1)}) fusion(f32[1024,128]{1,0:T(8,128)} %refs_2_.1, f32[1024,128]{1,0:T(8,128)} %refs_3_.1), kind=kLoop, calls=%fused_computation.4 | loop fusion | bytes 8192 | tf_op jit(solution)/shard_map/slice | solution.py:157
  2.8 0.7 %slice_bitcast_fusion = (f32[2,128]{1,0:T(2,128)S(1)}, f32[2,128]{1,0:T(2,128)S(1)}) fusion(f32[1,1024,128]{2,1,0:T(8,128)} %param.4), kind=kLoop, calls=%fused_computation.2 | loop fusion | bytes 4096 | tf_op jit(solution)/shard_map/slice | solution.py:157
  3.5 3.1 %collective-permute-start.1 = (f32[8,128]{1,0:T(8,128)S(1)}, f32[8,128]{1,0:T(8,128)S(1)}, u32[]{:S(2)}, u32[]{:S(2)}) collective-permute-start(f32[8,128]{1,0:T(8,128)S(1)} %pad_maximum_fusion), channel_id=1, source_target_pairs={{0,2},{1,3},{2,4},{3,5},{4,6},{5,7},{6,8},{7,9},{8,10},{9,11},{10,... | collective-permute-start | bytes 12296 | tf_op jit(solution)/shard_map/ppermute | solution.py:160
  6.7 0.1 pad.3.clone
  6.7 0.1 maximum_maximum_fusion
  6.8 3.9 %collective-permute-start.3 = (f32[8,128]{1,0:T(8,128)S(1)}, f32[8,128]{1,0:T(8,128)S(1)}, u32[]{:S(2)}, u32[]{:S(2)}) collective-permute-start(f32[8,128]{1,0:T(8,128)S(1)} %maximum_maximum_fusion), channel_id=1, source_target_pairs={{2,0},{3,1},{4,2},{5,3},{6,4},{7,5},{8,6},{9,7},{10,8},{11,9},{12,... | collective-permute-start | bytes 12296 | tf_op jit(solution)/shard_map/ppermute | solution.py:163
  10.8 2.6 %collective-permute-start.4 = (f32[2,128]{1,0:T(2,128)S(1)}, f32[2,128]{1,0:T(2,128)S(1)}, u32[]{:S(2)}, u32[]{:S(2)}) collective-permute-start(f32[2,128]{1,0:T(2,128)S(1)} %get-tuple-element.4), channel_id=1, source_target_pairs={{2,1},{3,0},{4,3},{5,2},{6,5},{7,4},{8,7},{9,6},{10,9},{11,8},{12,... | collective-permute-start | bytes 3080 | tf_op jit(solution)/shard_map/ppermute | solution.py:163
  13.4 2.9 %collective-permute-start.2 = (f32[2,128]{1,0:T(2,128)S(1)}, f32[2,128]{1,0:T(2,128)S(1)}, u32[]{:S(2)}, u32[]{:S(2)}) collective-permute-start(f32[2,128]{1,0:T(2,128)S(1)} %get-tuple-element.5), channel_id=1, source_target_pairs={{0,3},{1,2},{2,5},{3,4},{4,7},{5,6},{6,9},{7,8},{8,11},{9,10},{10,... | collective-permute-start | bytes 3080 | tf_op jit(solution)/shard_map/ppermute | solution.py:160
  16.3 0.0 collective-permute-done.4.refs_8_
  16.4 3.7 %collective-permute-done.2.refs_6_ = f32[2,128]{1,0:T(2,128)S(1)} collective-permute-done((f32[2,128]{1,0:T(2,128)S(1)}, f32[2,128]{1,0:T(2,128)S(1)}, u32[]{:S(2)}, u32[]{:S(2)}) %collective-permute-start.2) | collective-permute-done | bytes 1056 | tf_op jit(solution)/shard_map/ppermute | solution.py:160
  20.1 0.0 collective-permute-done.1.refs_5_
  20.1 0.0 collective-permute-done.3.refs_7_
  20.1 0.0 collective-permute-done.refs_1_
  20.1 0.0 copy-start
  20.1 1.0 %copy-done = f32[1,1024,128]{2,1,0:T(8,128)S(1)} copy-done((f32[1,1024,128]{2,1,0:T(8,128)S(1)}, f32[1,1024,128]{2,1,0:T(8,128)}, u32[]{:S(2)}) %copy-start) | copy-done | bytes 524312
  21.1 0.0 copy-start.1
  21.1 1.0 %copy-done.1 = f32[1024,128]{1,0:T(8,128)S(1)} copy-done((f32[1024,128]{1,0:T(8,128)S(1)}, f32[1024,128]{1,0:T(8,128)}, u32[]{:S(2)}) %copy-start.1) | copy-done | bytes 524312
  22.2 0.0 copy-start.2
  22.2 1.0 %copy-done.2 = f32[1024,128]{1,0:T(8,128)S(1)} copy-done((f32[1024,128]{1,0:T(8,128)S(1)}, f32[1024,128]{1,0:T(8,128)}, u32[]{:S(2)}) %copy-start.2) | copy-done | bytes 524312
  23.2 0.0 copy-start.3
  23.2 1.0 %copy-done.3 = f32[1024,128]{1,0:T(8,128)S(1)} copy-done((f32[1024,128]{1,0:T(8,128)S(1)}, f32[1024,128]{1,0:T(8,128)}, u32[]{:S(2)}) %copy-start.3) | copy-done | bytes 524312
  24.3 1.7 %precondition.1 = (f32[1024,128]{1,0:T(8,128)}, f32[1024,128]{1,0:T(8,128)}, f32[1024,128]{1,0:T(8,128)}, f32[1024,128]{1,0:T(8,128)}) custom-call(f32[1024,128]{1,0:T(8,128)S(1)} %bitcast.6, f32[1024,128]{1,0:T(8,128)S(1)} %collective-permute-done.refs_1_, f32[1024,128]{1,0:T(8,128)S(1)} %copy-done.1, f32[1024,128]{1,0:T(8,128)S(1)} %copy-done.2, ...), custom_call_target="tpu_custom_call" | custom-call | tf_op jit(solution)/shard_map/precondition/pallas_call | solution.py:173
  (2 shorter events, 0.0 us)
Async XLA Ops:
  0.6 19.5 %collective-permute-start = (f32[1024,128]{1,0:T(8,128)}, f32[1024,128]{1,0:T(8,128)S(1)}, u32[]{:S(2)}, u32[]{:S(2)}) collective-permute-start(f32[1024,128]{1,0:T(8,128)} %bitcast.5), channel_id=1, source_target_pairs={{0,1},{1,0},{2,3},{3,2},{4,5},{5,4},{6,7},{7,6},{8,9},{9,8},{10,11... | collective-permute-start | bytes 1572872 | tf_op jit(solution)/shard_map/ppermute | solution.py:165
  3.5 16.6 %collective-permute-start.1 = (f32[8,128]{1,0:T(8,128)S(1)}, f32[8,128]{1,0:T(8,128)S(1)}, u32[]{:S(2)}, u32[]{:S(2)}) collective-permute-start(f32[8,128]{1,0:T(8,128)S(1)} %pad_maximum_fusion), channel_id=1, source_target_pairs={{0,2},{1,3},{2,4},{3,5},{4,6},{5,7},{6,8},{7,9},{8,10},{9,11},{10,... | collective-permute-start | bytes 12296 | tf_op jit(solution)/shard_map/ppermute | solution.py:160
  6.8 13.3 %collective-permute-start.3 = (f32[8,128]{1,0:T(8,128)S(1)}, f32[8,128]{1,0:T(8,128)S(1)}, u32[]{:S(2)}, u32[]{:S(2)}) collective-permute-start(f32[8,128]{1,0:T(8,128)S(1)} %maximum_maximum_fusion), channel_id=1, source_target_pairs={{2,0},{3,1},{4,2},{5,3},{6,4},{7,5},{8,6},{9,7},{10,8},{11,9},{12,... | collective-permute-start | bytes 12296 | tf_op jit(solution)/shard_map/ppermute | solution.py:163
  10.8 5.6 %collective-permute-start.4 = (f32[2,128]{1,0:T(2,128)S(1)}, f32[2,128]{1,0:T(2,128)S(1)}, u32[]{:S(2)}, u32[]{:S(2)}) collective-permute-start(f32[2,128]{1,0:T(2,128)S(1)} %get-tuple-element.4), channel_id=1, source_target_pairs={{2,1},{3,0},{4,3},{5,2},{6,5},{7,4},{8,7},{9,6},{10,9},{11,8},{12,... | collective-permute-start | bytes 3080 | tf_op jit(solution)/shard_map/ppermute | solution.py:163
  13.4 6.7 %collective-permute-start.2 = (f32[2,128]{1,0:T(2,128)S(1)}, f32[2,128]{1,0:T(2,128)S(1)}, u32[]{:S(2)}, u32[]{:S(2)}) collective-permute-start(f32[2,128]{1,0:T(2,128)S(1)} %get-tuple-element.5), channel_id=1, source_target_pairs={{0,3},{1,2},{2,5},{3,4},{4,7},{5,6},{6,9},{7,8},{8,11},{9,10},{10,... | collective-permute-start | bytes 3080 | tf_op jit(solution)/shard_map/ppermute | solution.py:160
  20.1 1.0 %copy-start = (f32[1,1024,128]{2,1,0:T(8,128)S(1)}, f32[1,1024,128]{2,1,0:T(8,128)}, u32[]{:S(2)}) copy-start(f32[1,1024,128]{2,1,0:T(8,128)} %param.4) | copy-start | bytes 1572868
  21.1 1.0 %copy-start.1 = (f32[1024,128]{1,0:T(8,128)S(1)}, f32[1024,128]{1,0:T(8,128)}, u32[]{:S(2)}) copy-start(f32[1024,128]{1,0:T(8,128)} %refs_2_.1) | copy-start | bytes 1572868
  22.2 1.0 %copy-start.2 = (f32[1024,128]{1,0:T(8,128)S(1)}, f32[1024,128]{1,0:T(8,128)}, u32[]{:S(2)}) copy-start(f32[1024,128]{1,0:T(8,128)} %refs_3_.1) | copy-start | bytes 1572868
  23.2 1.0 %copy-start.3 = (f32[1024,128]{1,0:T(8,128)S(1)}, f32[1024,128]{1,0:T(8,128)}, u32[]{:S(2)}) copy-start(f32[1024,128]{1,0:T(8,128)} %refs_4_.1) | copy-start | bytes 1572868

commit v2 on v1

v2 whole, which is shorter than its diff:
```python
import functools

import jax
import jax.numpy as jnp
from jax import lax
from jax.experimental import pallas as pl
from jax.experimental.pallas import tpu as pltpu
from jax.sharding import PartitionSpec as P

decay_rate = 0.95
damping = 0.01
PAD = 8
TILE = 8


def solved(g, g1, g2, d, upper, lower, f, c, s):
    det = upper * lower - c * c
    n1 = lower * f - c * s
    n2 = upper * s - c * f
    schur = d * det - f * n1 - s * n2
    top = g * det - n1 * g1 - n2 * g2
    w = top / (schur * det)
    return w * det, w * n1, w * n2


def stage(count, *refs):
    sems = refs[2 * count]
    copies = [
        pltpu.make_async_copy(refs[k], refs[count + k], sems.at[k]) for k in range(count)
    ]
    for copy in copies:
        copy.start()
    for copy in copies:
        copy.wait()


def interior(parts, scale, rows, step, *refs):
    own = refs[:parts]
    diag_ref, first_ref, second_ref = refs[parts : parts + 3]
    outs = refs[parts + 3 : parts + 7]
    edges = refs[parts + 7]
    grad, diag, first, second, part1, part2, update, sems = refs[parts + 8 :]
    width = diag_ref.shape[1]
    chunks = rows // step
    end = PAD + rows

    zeros = jnp.zeros((PAD, width), jnp.float32)
    grad[end:, :] = zeros
    diag[end:, :] = zeros + 1.0
    first[end:, :] = zeros
    part1[:PAD, :] = zeros
    part2[:PAD, :] = zeros

    def gradients(c, carry):
        at = pl.multiple_of(c * step, step)
        here = pl.ds(at, step)
        there = pl.ds(at + PAD, step)
        g = own[0][here, :]
        for piece in own[1:]:
            g = g + piece[here, :]
        g = g * scale
        grad[there, :] = g
        diag[there, :] = decay_rate * diag_ref[here, :] + g * g
        return carry

    lax.fori_loop(0, chunks, gradients, 0, unroll=True)

    def bands(c, carry):
        at = pl.multiple_of(c * step, step)
        here = pl.ds(at, step)
        there = pl.ds(at + PAD, step)
        g = grad[there, :]
        g1 = grad[pl.ds(at + PAD + 1, step), :]
        g2 = grad[pl.ds(at + PAD + 2, step), :]
        first[there, :] = decay_rate * first_ref[here, :] + g * g1
        second[there, :] = decay_rate * second_ref[here, :] + g * g2
        return carry

    lax.fori_loop(0, chunks, bands, 0, unroll=True)

    copies = []

    def send(source, k):
        copy = pltpu.make_async_copy(source, outs[k], sems.at[k])
        copy.start()
        copies.append(copy)

    send(diag.at[PAD:end, :], 1)
    send(first.at[PAD:end, :], 2)
    send(second.at[PAD:end, :], 3)

    def values(c, carry):
        at = pl.multiple_of(c * step, step)
        there = pl.ds(at + PAD, step)
        after = pl.ds(at + PAD + 1, step)
        later = pl.ds(at + PAD + 2, step)
        v, p1, p2 = solved(
            grad[there, :],
            grad[after, :],
            grad[later, :],
            diag[there, :] + damping,
            diag[after, :] + damping,
            diag[later, :] + damping,
            first[there, :],
            first[after, :],
            second[there, :],
        )
        part1[there, :] = p1
        part2[there, :] = p2
        update[pl.ds(at, step), :] = (
            v - part1[pl.ds(at + PAD - 1, step), :] - part2[pl.ds(at + PAD - 2, step), :]
        )
        return carry

    lax.fori_loop(0, chunks, values, 0, unroll=True)
    send(update, 0)
    tops = [grad[PAD : PAD + TILE, :], diag[PAD : PAD + TILE, :], first[PAD : PAD + TILE, :]]
    tops.append(update[:TILE, :])
    tails = [r[end - TILE : end, :] for r in (grad, diag, first, second)]
    tails.append(update[rows - TILE :, :])
    tails += [r[end - TILE : end, :] for r in (part1, part2)]
    for k, tile in enumerate(tops + tails):
        edges[k * TILE : (k + 1) * TILE, :] = tile
    for copy in copies:
        copy.wait()


def border(rows, shards, paired, *refs):
    edges, got, other = refs[:3]
    outs = refs[6:9]
    work, tiles, sems = refs[9:]

    def edge(k, at, size):
        return edges[k * TILE + at : k * TILE + at + size, :]

    shard = lax.axis_index("fsdp")
    if paired:
        low = lax.axis_index("replica") == 0
        before = jnp.where(low, got[...], other[...])
        after = jnp.where(low, other[...], got[...])
    else:
        before, after = got[...], other[...]
    work[0:8, :] = jnp.where(shard == 0, 0.0, before)
    work[8:16, :] = jnp.where(shard == shards - 1, 0.0, after)

    g = work[0:2, :]
    g_next = edge(0, 0, 2)
    d = decay_rate * work[2:4, :] + g * g + damping
    d_next = edge(1, 0, 2) + damping
    g1 = jnp.concatenate([g[1:2], g_next[0:1]])
    d1 = jnp.concatenate([d[1:2], d_next[0:1]])
    f = decay_rate * work[4:6, :] + g * g1
    s = decay_rate * work[6:8, :] + g * g_next
    c = jnp.concatenate([f[1:2], edge(2, 0, 1)])
    _, p1, p2 = solved(g, g1, g_next, d, d1, d_next, f, c, s)
    tiles[0:8, :] = edges[3 * TILE : 4 * TILE, :]
    tiles[0:1, :] = tiles[0:1, :] - p1[1:2] - p2[0:1]
    tiles[1:2, :] = tiles[1:2, :] - p2[1:2]

    g = edge(4, 6, 2)
    g_next = work[8:10, :]
    present = work[14:16, :]
    d = edge(5, 6, 2) + damping
    d_next = (
        decay_rate * work[10:12, :] + g_next * g_next + present * damping + (1.0 - present)
    )
    g1 = jnp.concatenate([g[1:2], g_next[0:1]])
    d1 = jnp.concatenate([d[1:2], d_next[0:1]])
    f_last = (edge(6, 7, 1) + g[1:2] * g_next[0:1]) * present[0:1]
    f = jnp.concatenate([edge(6, 6, 1), f_last])
    s = (edge(7, 6, 2) + g * g_next) * present
    f_next = decay_rate * work[12:13, :] + g_next[0:1] * g_next[1:2]
    c = jnp.concatenate([f_last, f_next])
    v, p1, _ = solved(g, g1, g_next, d, d1, d_next, f, c, s)
    tiles[8:16, :] = edges[8 * TILE : 9 * TILE, :]
    tiles[14:15, :] = v[0:1] - edge(9, 5, 1) - edge(10, 4, 1)
    tiles[15:16, :] = v[1:2] - p1[0:1] - edge(10, 5, 1)
    tiles[16:24, :] = edges[6 * TILE : 7 * TILE, :]
    tiles[23:24, :] = f_last
    tiles[24:32, :] = edges[7 * TILE : 8 * TILE, :]
    tiles[30:32, :] = s

    copies = [
        pltpu.make_async_copy(tiles.at[0:8, :], outs[0].at[0:TILE, :], sems.at[0]),
        pltpu.make_async_copy(tiles.at[8:16, :], outs[0].at[rows - TILE : rows, :], sems.at[1]),
        pltpu.make_async_copy(tiles.at[16:24, :], outs[1].at[rows - TILE : rows, :], sems.at[2]),
        pltpu.make_async_copy(tiles.at[24:32, :], outs[2].at[rows - TILE : rows, :], sems.at[3]),
    ]
    for copy in copies:
        copy.start()
    for copy in copies:
        copy.wait()


def body(partials, diag_stat, first_stat, second_stat):
    own = partials[0]
    rows, width = own.shape
    replicas = lax.axis_size("replica")
    shards = lax.axis_size("fsdp")
    scale = 1.0 / replicas
    core = lax.axis_index("replica")
    paired = replicas == 2

    shape = jax.ShapeDtypeStruct((rows, width), jnp.float32)
    vmem = pl.BlockSpec(memory_space=pltpu.VMEM)
    hbm = pl.BlockSpec(memory_space=pltpu.HBM)
    params = pltpu.CompilerParams(vmem_limit_bytes=16 * 2**20)

    def swap(block):
        return lax.ppermute(block, "replica", [(0, 1), (1, 0)])

    if paired:
        pieces = [own, swap(own)]
    else:
        pieces = [lax.psum(own, "replica")]
    parts = len(pieces)

    moved = [own] * (parts - 1) + [diag_stat, first_stat, second_stat]
    count = len(moved)
    staged = pl.pallas_call(
        functools.partial(stage, count),
        out_shape=(shape,) * count,
        in_specs=[hbm] * count,
        out_specs=(vmem,) * count,
        scratch_shapes=[pltpu.SemaphoreType.DMA((count,))],
        compiler_params=pltpu.CompilerParams(vmem_limit_bytes=51 * 2**20),
        cost_estimate=pl.CostEstimate(
            flops=0, bytes_accessed=4 * count * rows * width, transcendentals=0
        ),
        name="stage",
    )(*moved)
    if paired:
        pieces[0] = staged[0]
    diag_in, first_in, second_in = staged[-3:]

    def edge(at):
        return sum(p[at : at + 2] for p in pieces) * scale

    ones = jnp.ones((2, width), jnp.float32)
    tail = rows - 2
    last = jnp.concatenate([edge(tail), diag_in[tail:], first_in[tail:], second_in[tail:]])
    head = jnp.concatenate([edge(0), diag_in[:2], first_in[:2], ones])
    if paired:
        up = [(2 * i, 2 * i + 2) for i in range(shards - 1)]
        down = [(2 * i + 1, 2 * i - 1) for i in range(1, shards)]
        turns = [(2 * shards - 2, 2 * shards - 1), (1, 0)]
        got = lax.ppermute(
            jnp.where(core == 0, last, head), ("fsdp", "replica"), up + down + turns
        )
        other = swap(got)
    else:
        got = lax.ppermute(last, "fsdp", [(i, i + 1) for i in range(shards - 1)])
        other = lax.ppermute(head, "fsdp", [(i + 1, i) for i in range(shards - 1)])

    padded = pltpu.VMEM((rows + 2 * PAD, width), jnp.float32)
    step = 64 if rows % 64 == 0 else 8
    update, diag_next, first_next, second_next, edges = pl.pallas_call(
        functools.partial(interior, parts, scale, rows, step),
        out_shape=(shape,) * 4 + (jax.ShapeDtypeStruct((11 * TILE, width), jnp.float32),),
        in_specs=[vmem] * (parts + 3),
        out_specs=(hbm,) * 4 + (vmem,),
        scratch_shapes=[padded] * 6
        + [pltpu.VMEM((rows, width), jnp.float32), pltpu.SemaphoreType.DMA((4,))],
        compiler_params=params,
        cost_estimate=pl.CostEstimate(
            flops=45 * rows * width, bytes_accessed=16 * rows * width, transcendentals=0
        ),
        name="interior",
    )(*pieces, diag_in, first_in, second_in)

    update, first_next, second_next = pl.pallas_call(
        functools.partial(border, rows, shards, paired),
        out_shape=(shape,) * 3,
        in_specs=[vmem] * 3 + [hbm] * 3,
        out_specs=(hbm,) * 3,
        input_output_aliases={3: 0, 4: 1, 5: 2},
        scratch_shapes=[
            pltpu.VMEM((16, width), jnp.float32),
            pltpu.VMEM((32, width), jnp.float32),
            pltpu.SemaphoreType.DMA((4,)),
        ],
        compiler_params=params,
        name="border",
    )(edges, got, other, update, first_next, second_next)
    return update, diag_next, first_next, second_next


def solution(mesh):
    return jax.shard_map(
        body,
        mesh=mesh,
        in_specs=(P("replica", "fsdp", None), P("fsdp", None), P("fsdp", None), P("fsdp", None)),
        out_specs=(P("fsdp", None), P("fsdp", None), P("fsdp", None), P("fsdp", None)),
        check_vma=False,
    )
```

time: 26.4 us -> 12.1 us (0.46)
  starting transfers between devices: 13.4 us -> 5.41 us
  local copies, waits for them, and re-layouts: 6.37 us -> 1.13 us
  waiting for transfers between devices: 3.74 us -> 0.76 us
  Pallas kernels: 1.69 us -> 3.81 us
    ppermute x5 -> x3, starting transfers between devices: 13.4 us -> 5.41 us  [the longest x2 3.36 us: swap(): return lax.ppermute(block, 'replica', [(0, 1), (1, 0)])]
    unnamed x8 -> x2, local copies, waits for them, and re-layouts: 4.16 us -> 1.04 us
    ppermute x5 -> x3, waiting for transfers between devices: 3.74 us -> 0.76 us  [the longest x1 0.75 us: body(): lax.ppermute(jnp.where(core == 0, last, head), ('fsdp', 'replica'), up +...]
    slice x3 -> x2, local copies, waits for them, and re-layouts: 2.13 us -> 0.01 us  [the longest x1 0.01 us: body(): second_in[tail:]]
    pallas_call x1 -> x3, Pallas kernels: 1.69 us -> 3.81 us  [the longest x1 1.69 us: body(): pl.pallas_call(functools.partial(interior, parts, scale, rows, step), out...]
  transfers between devices with their start and end apart: 5 -> 3, of which waited for: 1 -> 1; matrix products, arithmetic and copies ran while one was open for 9% -> 1% of each run, Pallas kernels for 0% -> 26%
where the time goes in v2:
time: 12.1 us; the launch traced here: 11.9 us
  starting transfers between devices  5.41 us (45%)
  Pallas kernels  3.81 us (31%)
  local copies, waits for them, and re-layouts  1.13 us (9%)
  waiting for transfers between devices  0.76 us (6%)
  between operations  0.68 us (6%)
    ppermute x2, starting transfers between devices, swap(): return lax.ppermute(block, 'replica', [(0, 1), (1, 0)])  3.36 us
    ppermute x1, starting transfers between devices, body(): lax.ppermute(jnp.where(core == 0, last, head), ('fsdp', 'replica'), up +...  2.06 us
    pallas_call x1, Pallas kernels, body(): pl.pallas_call(functools.partial(interior, parts, scale, rows, step), out...  1.69 us
    pallas_call x1, Pallas kernels, body(): pl.pallas_call(functools.partial(stage, count), out_shape=(shape,) * coun...  1.43 us
    unnamed x2, local copies, waits for them, and re-layouts  1.04 us
    ppermute x1, waiting for transfers between devices, body(): lax.ppermute(jnp.where(core == 0, last, head), ('fsdp', 'replica'), up +...  0.75 us
    pallas_call x1, Pallas kernels, body(): pl.pallas_call(functools.partial(border, rows, shards, paired), out_shape...  0.69 us
  transfers between devices with their start and end apart: 3, of which 1 were waited for; matrix products, arithmetic and copies ran while one was open for 1% of the time, Pallas kernels for 26%

profile of v2, /device:TPU:9, one launch (start us, length us, event | category | flops | bytes accessed | tf_op | source)
XLA Modules:
  0.0 11.9 jit_solution(8965890398395898186)
XLA Ops:
  0.6 0.7 %collective-permute-start = (f32[1024,128]{1,0:T(8,128)}, f32[1024,128]{1,0:T(8,128)S(1)}, u32[]{:S(2)}, u32[]{:S(2)}) collective-permute-start(f32[1024,128]{1,0:T(8,128)} %bitcast.1), channel_id=1, source_target_pairs={{0,1},{1,0},{2,3},{3,2},{4,5},{5,4},{6,7},{7,6},{8,9},{9,8},{10,11... | collective-permute-start | bytes 1572872 | tf_op jit(solution)/shard_map/ppermute | solution.py:210
  1.4 0.0 copy-start
  1.4 1.0 %copy-done = f32[1,1024,128]{2,1,0:T(8,128)S(1)} copy-done((f32[1,1024,128]{2,1,0:T(8,128)S(1)}, f32[1,1024,128]{2,1,0:T(8,128)}, u32[]{:S(2)}) %copy-start) | copy-done | bytes 524312
  2.4 1.4 %stage.1 = (f32[1024,128]{1,0:T(8,128)S(1)}, f32[1024,128]{1,0:T(8,128)S(1)}, f32[1024,128]{1,0:T(8,128)S(1)}, f32[1024,128]{1,0:T(8,128)S(1)}) custom-call(f32[1024,128]{1,0:T(8,128)S(1)} %bitcast.2, f32[1024,128]{1,0:T(8,128)} %refs_1_.1, f32[1024,128]{1,0:T(8,128)} %refs_2_.1, f32[1024,128]{1,0:T(8,128)} %refs_3_.1), custom_call_target="tpu_custom_call" | custom-call | bytes 2097152 | tf_op jit(solution)/shard_map/stage/pallas_call | solution.py:220
  3.9 0.1 pad.3.clone
  4.0 0.0 collective-permute-done.refs_1_
  4.0 0.1 maximum_select_fusion
  4.0 2.1 %collective-permute-start.1 = (f32[8,128]{1,0:T(8,128)S(1)}, f32[8,128]{1,0:T(8,128)S(1)}, u32[]{:S(2)}, u32[]{:S(2)}) collective-permute-start(f32[8,128]{1,0:T(8,128)S(1)} %maximum_select_fusion), channel_id=1, source_target_pairs={{0,2},{2,4},{4,6},{6,8},{8,10},{10,12},{12,14},{14,16},{16,18},{18... | collective-permute-start | bytes 12296 | tf_op jit(solution)/shard_map/ppermute | solution.py:247
  6.1 0.8 %collective-permute-done.1.refs_1_ = f32[8,128]{1,0:T(8,128)S(1)} collective-permute-done((f32[8,128]{1,0:T(8,128)S(1)}, f32[8,128]{1,0:T(8,128)S(1)}, u32[]{:S(2)}, u32[]{:S(2)}) %collective-permute-start.1) | collective-permute-done | bytes 4128 | tf_op jit(solution)/shard_map/ppermute | solution.py:247
  6.9 2.6 %collective-permute-start.2 = (f32[8,128]{1,0:T(8,128)S(1)}, f32[8,128]{1,0:T(8,128)S(1)}, u32[]{:S(2)}, u32[]{:S(2)}) collective-permute-start(f32[8,128]{1,0:T(8,128)S(1)} %collective-permute-done.1.refs_1_), channel_id=1, source_target_pairs={{0,1},{1,0},{2,3},{3,2},{4,5},{5,4},{6,7},{7,6},{8,9},{9,8},{10,11... | collective-permute-start | bytes 12296 | tf_op jit(solution)/shard_map/ppermute | solution.py:210
  9.5 1.7 %interior.1 = (f32[1024,128]{1,0:T(8,128)}, f32[1024,128]{1,0:T(8,128)}, f32[1024,128]{1,0:T(8,128)}, f32[1024,128]{1,0:T(8,128)}, f32[88,128]{1,0:T(8,128)S(1)}) custom-call(f32[1024,128]{1,0:T(8,128)S(1)} %get-tuple-element.16.refs_0_, f32[1024,128]{1,0:T(8,128)S(1)} %collective-permute-done.refs_1_, f32[1024,128]{1,0:T(8,128)S(1)} %get-tuple-element.17.refs_2_, ...), custom_call_target="tpu_custom_call" | custom-call | flops 5898240 | bytes 2097152 | tf_op jit(solution)/shard_map/interior/pallas_call | solution.py:257
  11.2 0.0 collective-permute-done.2.refs_2_
  11.2 0.7 %border.1 = (f32[1024,128]{1,0:T(8,128)}, f32[1024,128]{1,0:T(8,128)}, f32[1024,128]{1,0:T(8,128)}) custom-call(f32[88,128]{1,0:T(8,128)S(1)} %get-tuple-element.20.refs_0_, f32[8,128]{1,0:T(8,128)S(1)} %collective-permute-done.1.refs_1_, f32[8,128]{1,0:T(8,128)S(1)} %collective-permute-done.2.refs_2_, ...), custom_call_target="tpu_custom_call", output_to_operand_aliasing={{0}: (3, {}), {1}: (4, {}), {2}: (5, {})} | custom-call | tf_op jit(solution)/shard_map/border/pallas_call | solution.py:271
  (4 shorter events, 0.0 us)
Async XLA Ops:
  0.6 3.3 %collective-permute-start = (f32[1024,128]{1,0:T(8,128)}, f32[1024,128]{1,0:T(8,128)S(1)}, u32[]{:S(2)}, u32[]{:S(2)}) collective-permute-start(f32[1024,128]{1,0:T(8,128)} %bitcast.1), channel_id=1, source_target_pairs={{0,1},{1,0},{2,3},{3,2},{4,5},{5,4},{6,7},{7,6},{8,9},{9,8},{10,11... | collective-permute-start | bytes 1572872 | tf_op jit(solution)/shard_map/ppermute | solution.py:210
  1.4 1.0 %copy-start = (f32[1,1024,128]{2,1,0:T(8,128)S(1)}, f32[1,1024,128]{2,1,0:T(8,128)}, u32[]{:S(2)}) copy-start(f32[1,1024,128]{2,1,0:T(8,128)} %param.4) | copy-start | bytes 1572868
  4.0 2.8 %collective-permute-start.1 = (f32[8,128]{1,0:T(8,128)S(1)}, f32[8,128]{1,0:T(8,128)S(1)}, u32[]{:S(2)}, u32[]{:S(2)}) collective-permute-start(f32[8,128]{1,0:T(8,128)S(1)} %maximum_select_fusion), channel_id=1, source_target_pairs={{0,2},{2,4},{4,6},{6,8},{8,10},{10,12},{12,14},{14,16},{16,18},{18... | collective-permute-start | bytes 12296 | tf_op jit(solution)/shard_map/ppermute | solution.py:247
  6.9 4.3 %collective-permute-start.2 = (f32[8,128]{1,0:T(8,128)S(1)}, f32[8,128]{1,0:T(8,128)S(1)}, u32[]{:S(2)}, u32[]{:S(2)}) collective-permute-start(f32[8,128]{1,0:T(8,128)S(1)} %collective-permute-done.1.refs_1_), channel_id=1, source_target_pairs={{0,1},{1,0},{2,3},{3,2},{4,5},{5,4},{6,7},{7,6},{8,9},{9,8},{10,11... | collective-permute-start | bytes 12296 | tf_op jit(solution)/shard_map/ppermute | solution.py:210
